TPU v7x, 32 devices: a whole 2x2x4 slice. The times are simulated.
32 devices in a mesh: expert: 8 (over z, y), tensor: 4 (over x, core).
Axes of the slice: x: 2, y: 2, z: 4, core: 2. Of those that a mesh axis runs over, the one named last changes fastest.
Arguments:
- tokens: bfloat16 [1024, 2048], P('expert', 'tensor'), may hold values from -6 to 6
- labels: int32 [1024, 1], P('expert'), may hold values from 0 to 3, as said below
- domain_ids: int32 [1024], P('expert'), may hold values from 0 to 21
- domain_weights: float32 [22], replicated, may hold values from 0.02 to 0.5
- cotangent: bfloat16 [1024, 2048], P('expert', 'tensor'), may hold values from -6 to 6
- gate_weight: bfloat16 [8, 2048, 2048], P('expert', None, 'tensor'), may hold values from -0.125 to 0.125
- up_weight: bfloat16 [8, 2048, 2048], P('expert', None, 'tensor'), may hold values from -0.125 to 0.125
- down_weight: bfloat16 [8, 2048, 2048], P('expert', 'tensor'), may hold values from -0.09375 to 0.09375
Outputs:
- layer_out: bfloat16 [1024, 2048], P('expert', 'tensor')
- input_grad: bfloat16 [1024, 2048], P('expert', 'tensor')
- gate_grad: bfloat16 [8, 2048, 2048], P('expert', None, 'tensor')
- up_grad: bfloat16 [8, 2048, 2048], P('expert', None, 'tensor')
- down_grad: bfloat16 [8, 2048, 2048], P('expert', 'tensor')
Inputs may be any that keep to these rules, and one draw needn't show every extreme that they name: `labels`: among the rows of one device (aligned blocks of 128 rows) no label appears more than 64 times, and every such block has some label exactly 64 times.
All inputs are finite; a program needn't handle non-finite values.
Results may differ from a plain program's by a relative error of at most 0.0058.
Values may be sent and summed in bfloat16 or wider, within the bound.
A program may use at most 320 MiB of HBM per device.

v0:
```python
import jax
import jax.numpy as jnp
from jax import lax
from jax.sharding import PartitionSpec as P

SPLIT = 2


def partner(value, axis, stride):
    return lax.ppermute(value, axis, [(i, i ^ 1 << stride) for i in range(lax.axis_size(axis))])


def silu_parts(gate_pre):
    squash = jax.nn.sigmoid(gate_pre)
    return (squash, gate_pre * squash)


def body(
    tokens, labels, domain_ids, domain_weights, cotangent, gate_weight, up_weight, down_weight
):
    n_expert = lax.axis_size("expert")
    tok_rows = tokens.shape[0]
    experts_all = n_expert // SPLIT
    capacity = 2 * tok_rows // experts_all
    half_cap = capacity // 2
    parity = lax.axis_index("expert") % 2
    lang_label = labels[:, 0]
    dom_hot = (
        domain_ids[:, None] == jnp.arange(domain_weights.shape[0], dtype=jnp.int32)[None, :]
    ).astype(jnp.float32)
    tok_scale = jnp.sum(dom_hot * domain_weights[None, :], axis=1)
    grad_rows = (tok_scale[:, None] * cotangent.astype(jnp.float32)).astype(jnp.bfloat16)
    lab_hot = (lang_label[:, None] == jnp.arange(experts_all, dtype=jnp.int32)[None, :]).astype(
        jnp.float32
    )
    row_ids = jnp.arange(tok_rows, dtype=jnp.int32)
    earlier = (row_ids[None, :] < row_ids[:, None]).astype(jnp.float32)
    before = jnp.dot(earlier, lab_hot, precision=lax.Precision.HIGHEST)
    slot_pos = jnp.sum(before * lab_hot, axis=1).astype(jnp.int32)
    target_row = lang_label * capacity + slot_pos
    sources = jnp.stack((tokens, grad_rows))
    sources = lax.all_gather(sources, "tensor", axis=2, tiled=True)
    slot_ids = jnp.arange(n_expert * capacity, dtype=jnp.int32)
    dispatch_map = (slot_ids[:, None] // capacity // SPLIT == lang_label[None, :]) & (
        slot_ids[:, None] % capacity == slot_pos[None, :]
    )
    dispatch_map = dispatch_map.astype(jnp.bfloat16)
    outbound = jnp.einsum(
        "rt,ktw->krw", dispatch_map, sources, preferred_element_type=jnp.float32
    ).astype(jnp.bfloat16)
    outbound = outbound.reshape(2, n_expert, capacity, sources.shape[2])
    arrived = lax.all_to_all(outbound, "expert", split_axis=1, concat_axis=1, tiled=True)
    rows_all = n_expert * capacity
    feat_width = arrived.shape[3]
    routed = arrived[0].reshape(rows_all, feat_width)
    routed_grad = arrived[1].reshape(rows_all, feat_width)
    w_gate = gate_weight[0]
    w_up = up_weight[0]
    w_down = down_weight[0]
    contract_rows = (((0,), (0,)), ((), ()))
    contract_cols = (((1,), (1,)), ((), ()))
    gate_pre = jnp.dot(routed, w_gate, preferred_element_type=jnp.float32)
    up_pre = jnp.dot(routed, w_up, preferred_element_type=jnp.float32)
    squash, activated = silu_parts(gate_pre)
    hidden = (activated * up_pre).astype(jnp.bfloat16)
    out_part = jnp.dot(hidden, w_down, preferred_element_type=jnp.float32)
    grad_hidden = lax.dot_general(
        routed_grad, w_down, contract_cols, preferred_element_type=jnp.float32
    )
    grad_gate_pre = (grad_hidden * up_pre * squash * (1.0 + gate_pre * (1.0 - squash))).astype(
        jnp.bfloat16
    )
    grad_up_pre = (grad_hidden * activated).astype(jnp.bfloat16)
    gate_grad = lax.dot_general(
        routed, grad_gate_pre, contract_rows, preferred_element_type=jnp.float32
    ).astype(jnp.bfloat16)[None]
    up_grad = lax.dot_general(
        routed, grad_up_pre, contract_rows, preferred_element_type=jnp.float32
    ).astype(jnp.bfloat16)[None]
    down_grad = lax.dot_general(
        hidden, routed_grad, contract_rows, preferred_element_type=jnp.float32
    ).astype(jnp.bfloat16)[None]
    input_part = lax.dot_general(
        grad_gate_pre, w_gate, contract_cols, preferred_element_type=jnp.float32
    ) + lax.dot_general(grad_up_pre, w_up, contract_cols, preferred_element_type=jnp.float32)
    out_part = out_part.reshape(n_expert, capacity, feat_width)
    input_part = input_part.reshape(n_expert, capacity, feat_width)
    out_share, input_share = (
        lax.psum_scatter(out_part, "tensor", scatter_dimension=2, tiled=True),
        lax.psum_scatter(input_part, "tensor", scatter_dimension=2, tiled=True),
    )
    partial_value = jnp.stack((out_share, input_share))
    kept = jnp.where(parity == 0, partial_value[:, :, :half_cap], partial_value[:, :, half_cap:])
    handed = jnp.where(parity == 0, partial_value[:, :, half_cap:], partial_value[:, :, :half_cap])
    summed = kept + partner(handed, "expert", 0)
    going_back = summed.astype(jnp.bfloat16)
    returned = lax.all_to_all(going_back, "expert", split_axis=1, concat_axis=1, tiled=True)
    home_ids = jnp.arange(n_expert * half_cap, dtype=jnp.int32)
    home_map = (home_ids[:, None] == target_row[None, :]).astype(jnp.bfloat16)
    flat_back = returned.reshape(2, n_expert * half_cap, returned.shape[3])
    gathered_home = jnp.einsum(
        "rt,krw->ktw", home_map, flat_back, preferred_element_type=jnp.float32
    ).astype(jnp.bfloat16)
    return (gathered_home[0], gathered_home[1], gate_grad, up_grad, down_grad)


def solution(mesh):
    return jax.shard_map(
        body,
        mesh=mesh,
        in_specs=(
            P("expert", "tensor"),
            P("expert", None),
            P("expert"),
            P(),
            P("expert", "tensor"),
            P("expert", None, "tensor"),
            P("expert", None, "tensor"),
            P("expert", "tensor", None),
        ),
        out_specs=(
            P("expert", "tensor"),
            P("expert", "tensor"),
            P("expert", None, "tensor"),
            P("expert", None, "tensor"),
            P("expert", "tensor", None),
        ),
        check_vma=False,
    )
```

profile of v0, /device:TPU:0, one launch (start us, length us, event | category | flops | bytes accessed | tf_op | source)
XLA Modules:
  0.0 289.5 jit_solution(6542582623687329574)
XLA Ops:
  7.2 0.9 select_reduce_fusion
  8.1 1.0 fusion.22
  9.1 1.6 pad_maximum_fusion.1
  10.8 0.9 fusion.15
  11.7 18.7 %all-gather.2.cloned.1.call-done = bf16[2,128,2048]{2,1,0:T(8,128)(2,1)} async-done(((bf16[2,128,512]{2,1,0:T(8,128)(2,1)}), bf16[2,128,2048]{2,1,0:T(8,128)(2,1)}) %all-gather.2.cloned.1.call-update) | async-done | bytes 1048592 | tf_op jit(solution)/shard_map/all_gather | solution.py:42
  30.4 2.5 convolution_convert_fusion
  33.5 98.8 %all_to_all.10 = bf16[2,8,64,2048]{3,2,0,1:T(8,128)(2,1)S(1)} all-to-all(bf16[2,8,64,2048]{3,2,0,1:T(8,128)(2,1)S(1)} %copy.27), channel_id=1, replica_groups=mesh['expert'=8,'tensor'=4] {'expert'}, dimensions={1} | all-to-all | bytes 8388608 | tf_op jit(solution)/shard_map/all_to_all | solution.py:52
  132.9 1.0 copy-done.3
  134.0 1.2 fusion.12
  136.0 1.4 fusion.5
  137.4 1.7 multiply_convert_fusion.2
  139.1 1.3 fusion.10
  140.4 3.3 %convolution_add_fusion = f32[512,2048]{1,0:T(8,128)} fusion(f32[512,2048]{1,0:T(8,128)S(1)} %fusion.10, bf16[512,512]{1,0:T(8,128)(2,1)S(1)} %get-tuple-element.29, bf16[1,2048,512]{2,1,0:T(8,128)(2,1)S(1)} %copy-done), kind=kOutput, calls=%fused_computation.1 | convolution fusion | flops 1074790400 | bytes 11010048 | tf_op jit(solution)/shard_map/dot_general | solution.py:85
  143.8 4.8 %fusion.3 = f32[8,64,2048]{2,1,0:T(8,128)} fusion(bf16[8,64,512]{2,1,0:T(8,128)(2,1)S(1)} %bitcast.78, bf16[1,512,2048]{2,1,0:T(8,128)(2,1)} %param.15), kind=kOutput, calls=%fused_computation.10 | convolution fusion | flops 1073741824 | bytes 6815744 | tf_op jit(solution)/shard_map/dot_general | solution.py:66
  148.7 37.8 %reduce-scatter.5.cloned.1.call-done = f32[8,64,512]{2,1,0:T(8,128)} async-done(((f32[8,64,2048]{2,1,0:T(8,128)}), f32[8,64,512]{2,1,0:T(8,128)}) %reduce-scatter.5.cloned.1.call-update) | async-done | bytes 1048592 | tf_op jit(solution)/shard_map/reduce_scatter | solution.py:90
  186.5 47.2 %reduce-scatter.3.cloned.1.call-done = f32[8,64,512]{2,1,0:T(8,128)} async-done(((f32[8,64,2048]{2,1,0:T(8,128)}), f32[8,64,512]{2,1,0:T(8,128)}) %reduce-scatter.3.cloned.1.call-update) | async-done | bytes 1048592 | tf_op jit(solution)/shard_map/reduce_scatter | solution.py:89
  233.8 1.8 broadcast_select_fusion
  235.6 1.5 collective-permute-start
  237.2 23.4 %collective-permute-done = f32[2,8,32,512]{3,2,1,0:T(8,128)S(1)} collective-permute-done((f32[2,8,32,512]{3,2,1,0:T(8,128)S(1)}, f32[2,8,32,512]{3,2,1,0:T(8,128)S(1)}, u32[]{:S(2)}, u32[]{:S(2)}) %collective-permute-start) | collective-permute-done | bytes 1048608 | tf_op jit(solution)/shard_map/ppermute | solution.py:10
  261.8 5.5 %all-to-all-start.1 = ((bf16[2,8,32,512]{3,2,0,1:T(8,128)(2,1)}), bf16[2,8,32,512]{3,2,0,1:T(8,128)(2,1)S(1)}, u32[]{:S(2)}, u32[]{:S(2)}) async-start(bf16[2,8,32,512]{3,2,0,1:T(8,128)(2,1)} %copy.28), calls=%async_computation.3 | async-start | bytes 1048576 | tf_op jit(solution)/shard_map/all_to_all | solution.py:97
  267.4 4.4 %fusion = bf16[1,2048,512]{2,1,0:T(8,128)(2,1)} fusion(bf16[512,2048]{1,0:T(8,128)(2,1)} %bitcast.76, bf16[512,512]{1,0:T(8,128)(2,1)} %copy-done.11), kind=kOutput, calls=%fused_computation.5 | convolution fusion | flops 1074790400 | bytes 4718592 | tf_op jit(solution)/shard_map/dot_general | solution.py:74
  271.8 2.6 fusion.1
  274.4 2.6 fusion.2
  277.0 4.0 %all-to-all-done.1 = bf16[2,8,32,512]{3,2,0,1:T(8,128)(2,1)S(1)} async-done(((bf16[2,8,32,512]{3,2,0,1:T(8,128)(2,1)}), bf16[2,8,32,512]{3,2,0,1:T(8,128)(2,1)S(1)}, u32[]{:S(2)}, u32[]{:S(2)}) %all-to-all-start.1) | async-done | bytes 524320 | tf_op jit(solution)/shard_map/all_to_all | solution.py:97
  (47 shorter events, 5.3 us)
Async XLA Ops:
  7.2 130.2 %copy-start = (bf16[1,2048,512]{2,1,0:T(8,128)(2,1)S(1)}, bf16[1,2048,512]{2,1,0:T(8,128)(2,1)}, u32[]{:S(2)}) copy-start(bf16[1,2048,512]{2,1,0:T(8,128)(2,1)} %param.14) | copy-start | bytes 6291460
  7.2 23.2 %all-gather.2.cloned.1.call-start = ((), (), s32[]{:S(2)}) async-start(), calls=%async_computation.4 | async-start | bytes 1310720 | tf_op jit(solution)/shard_map/all_gather | solution.py:42
  10.8 175.8 %reduce-scatter.5.cloned.1.call-start = ((), (), s32[]{:S(2)}) async-start(), calls=%async_computation.6 | async-start | bytes 5242880 | tf_op jit(solution)/shard_map/reduce_scatter | solution.py:90
  132.3 1.6 copy-start.3
  132.9 2.3 copy-start.5
  132.9 4.4 %copy-start.7 = (bf16[1,8,64,2048]{3,2,0,1:T(8,128)(2,1)}, bf16[1,8,64,2048]{3,2,0,1:T(8,128)(2,1)S(1)}, u32[]{:S(2)}) copy-start(bf16[1,8,64,2048]{3,2,0,1:T(8,128)(2,1)S(1)} %get-tuple-element.26) | copy-start | bytes 6291460
  134.0 2.0 copy-start.4
  139.1 1.3 copy-start.11
  139.1 1.3 copy-start.12
  139.1 4.7 %copy-start.9 = (bf16[512,512]{1,0:T(8,128)(2,1)}, bf16[512,512]{1,0:T(8,128)(2,1)S(1)}, u32[]{:S(2)}) copy-start(bf16[512,512]{1,0:T(8,128)(2,1)S(1)} %get-tuple-element.27) | copy-start | bytes 1572868
  143.8 90.0 %reduce-scatter.3.cloned.1.call-start = ((), (), s32[]{:S(2)}) async-start(), calls=%async_computation.5 | async-start | bytes 5242880 | tf_op jit(solution)/shard_map/reduce_scatter | solution.py:89
  148.7 88.5 %copy-start.14 = (s32[128,1]{0,1:T(1,128)S(1)}, s32[128,1]{0,1:T(1,128)}, u32[]{:S(2)}) copy-start(s32[128,1]{0,1:T(1,128)} %param.9) | copy-start | bytes 1540
  186.5 74.1 %copy-start.1 = (f32[8,64,512]{2,1,0:T(8,128)S(1)}, f32[8,64,512]{2,1,0:T(8,128)}, u32[]{:S(2)}) copy-start(f32[8,64,512]{2,1,0:T(8,128)} %reduce-scatter.5.cloned.1.call-done) | copy-start | bytes 3145732
  233.8 26.8 %copy-start.2 = (f32[8,64,512]{2,1,0:T(8,128)S(1)}, f32[8,64,512]{2,1,0:T(8,128)}, u32[]{:S(2)}) copy-start(f32[8,64,512]{2,1,0:T(8,128)} %reduce-scatter.3.cloned.1.call-done) | copy-start | bytes 3145732
  235.6 25.0 %collective-permute-start = (f32[2,8,32,512]{3,2,1,0:T(8,128)S(1)}, f32[2,8,32,512]{3,2,1,0:T(8,128)S(1)}, u32[]{:S(2)}, u32[]{:S(2)}) collective-permute-start(f32[2,8,32,512]{3,2,1,0:T(8,128)S(1)} %broadcast_select_fusion), channel_id=1, source_target_pairs={{0,4},{4,0},{8,12},{12,8},{16,20},{20,16},{24,28},{28,24},{1,5},{5... | collective-permute-start | bytes 3145736 | tf_op jit(solution)/shard_map/ppermute | solution.py:10
  261.8 19.2 %all-to-all-start.1 = ((bf16[2,8,32,512]{3,2,0,1:T(8,128)(2,1)}), bf16[2,8,32,512]{3,2,0,1:T(8,128)(2,1)S(1)}, u32[]{:S(2)}, u32[]{:S(2)}) async-start(bf16[2,8,32,512]{3,2,0,1:T(8,128)(2,1)} %copy.28), calls=%async_computation.3 | async-start | bytes 1048576 | tf_op jit(solution)/shard_map/all_to_all | solution.py:97
  267.3 4.5 %copy-start.8 = (bf16[1,8,64,2048]{3,2,0,1:T(8,128)(2,1)S(1)}, bf16[1,8,64,2048]{3,2,0,1:T(8,128)(2,1)}, u32[]{:S(2)}) copy-start(bf16[1,8,64,2048]{3,2,0,1:T(8,128)(2,1)} %copy-done.7) | copy-start | bytes 6291460
  267.4 4.4 %copy-start.13 = (bf16[512,512]{1,0:T(8,128)(2,1)S(1)}, bf16[512,512]{1,0:T(8,128)(2,1)}, u32[]{:S(2)}) copy-start(bf16[512,512]{1,0:T(8,128)(2,1)} %copy-done.12) | copy-start | bytes 1572868
  271.8 2.6 copy-start.6
  271.8 2.6 copy-start.10
Sparse Core Ops, SparseCore 0:
  10.9 19.4 all-gather.1
  143.9 42.6 reduce-scatter.4
  189.2 44.5 reduce-scatter.2
where the time goes:
time: 290 us; the launch traced here: 289 us
  waiting for transfers between devices  131 us (45%)
  blocking collectives  98.8 us (34%)
  matrix products  27.2 us (9%)
  between operations  14 us (5%)
  starting transfers between devices  7.15 us (2%)
  other arithmetic  5.78 us (2%)
  local copies, waits for them, and re-layouts  5.37 us (2%)
    all_to_all x1, blocking collectives, body(): lax.all_to_all(outbound, 'expert', split_axis=1, concat_axis=1, tiled=True)  98.8 us
    reduce_scatter x1, waiting for transfers between devices, body(): lax.psum_scatter(out_part, 'tensor', scatter_dimension=2, tiled=True)  47.2 us
    reduce_scatter x1, waiting for transfers between devices, body(): lax.psum_scatter(input_part, 'tensor', scatter_dimension=2, tiled=True)  37.8 us
    ppermute x1, waiting for transfers between devices, partner(): lax.ppermute(value, axis, [(i, i ^ 1 << stride) for i in range(lax.axis_s...  23.4 us
    all_gather x1, waiting for transfers between devices, body(): sources = lax.all_gather(sources, 'tensor', axis=2, tiled=True)  18.7 us
  transfers between devices with their start and end apart: 5, of which 5 were waited for; matrix products, arithmetic and copies ran while one was open for 5% of the time, Pallas kernels for 0%

commit v1 on v0

--- a/solution.py
+++ b/solution.py
@@ -1,9 +1,18 @@
 import jax
 import jax.numpy as jnp
 from jax import lax
+from jax.experimental import pallas as pl
+from jax.experimental.pallas import tpu as pltpu
 from jax.sharding import PartitionSpec as P
 
 SPLIT = 2
+F32 = jnp.float32
+BF16 = jnp.bfloat16
+MESH = pl.DeviceIdType.MESH
+(
+    ZOUT, XOWN, YOWN, SOWN, FWDA, FWDB, SPX, SPY, SPD,
+    RSIB, RDA, RDB, RX, RY, RZ, KINDS,
+) = range(16)
 
 
 def partner(value, axis, stride):
@@ -104,9 +113,358 @@
     return (gathered_home[0], gathered_home[1], gate_grad, up_grad, down_grad)
 
 
+def expert_kernel(
+    tok_ref, cot_ref, lab_ref, dom_ref, dw_ref, wg_hbm, wu_hbm, wd_hbm,
+    y_ref, yg_ref, rows_hbm, hid_hbm, ggp_hbm, gup_hbm,
+    wg, wu, wd, slots, rows, gate_pre, up_pre, hidden, ggp, gup, keep,
+    sib_src, sib_dst, diag_src, diag_dst, nx_src, nx_dst, ny_src, ny_dst,
+    back_src, back, send_sem, recv_sem, local_sem,
+):
+    n_tok, width = tok_ref.shape
+    n_lang = slots.shape[0]
+    cap = slots.shape[2]
+    half = cap // 2
+    block = 2 * cap
+    ei = lax.axis_index("expert")
+    ti = lax.axis_index("tensor")
+    z, y = ei // 2, ei % 2
+    x, c = ti // 2, ti % 2
+    nx, ny = 1 - x, 1 - y
+    tix = nx * 2 + c
+    tis = x * 2 + 1 - c
+    tixs = nx * 2 + 1 - c
+    plane = [z, z + 1 - 2 * (z % 2), (z + 2) % 4, 3 - z]
+    x_dev, y_dev, s_dev = (ei, tix), (z * 2 + ny, ti), (ei, tis)
+    z_dev = [(plane[j] * 2 + y, ti) for j in range(n_lang)]
+
+    loads = [
+        pltpu.make_async_copy(wg_hbm.at[0], wg, local_sem.at[0]),
+        pltpu.make_async_copy(wu_hbm.at[0], wu, local_sem.at[1]),
+        pltpu.make_async_copy(wd_hbm.at[0], wd, local_sem.at[2]),
+    ]
+    barrier = pltpu.get_barrier_semaphore()
+    others = [x_dev, y_dev, s_dev] + z_dev[1:]
+    for dev in others:
+        pl.semaphore_signal(barrier, inc=1, device_id=dev, device_id_type=MESH)
+    for copy in loads:
+        copy.start()
+
+    lab = lab_ref[...]
+    lane = lax.broadcasted_iota(jnp.int32, (n_tok, n_tok), 1)
+    sub = lax.broadcasted_iota(jnp.int32, (n_tok, n_tok), 0)
+    lab_hot = jnp.where(lane == lab, 1.0, 0.0)
+    earlier = jnp.where(lane < sub, 1.0, 0.0).astype(BF16)
+    before = jnp.dot(earlier, lab_hot.astype(BF16), preferred_element_type=F32)
+    pos = jnp.sum(before * lab_hot, axis=1, keepdims=True)
+    target = lab.astype(F32) * cap + pos
+    slot_lane = lax.broadcasted_iota(jnp.int32, (n_tok, n_lang * cap), 1).astype(F32)
+    to_slot = jnp.where(slot_lane == target, 1.0, 0.0).astype(BF16)
+    dom_row = jnp.broadcast_to(dom_ref[...].astype(F32), (n_tok, n_tok))
+    dom_col = jnp.sum(jnp.where(lane == sub, dom_row, 0.0), axis=1, keepdims=True)
+    n_dom = dw_ref.shape[1]
+    dom_lane = lax.broadcasted_iota(jnp.int32, (n_tok, n_dom), 1).astype(F32)
+    dw_row = jnp.broadcast_to(dw_ref[...], (n_tok, n_dom))
+    scale = jnp.sum(jnp.where(dom_lane == dom_col, dw_row, 0.0), axis=1, keepdims=True)
+    grad_rows = (scale * cot_ref[...].astype(F32)).astype(BF16)
+    over_tokens = (((0,), (0,)), ((), ()))
+    for k, source in enumerate((tok_ref[...], grad_rows)):
+        packed = lax.dot_general(
+            to_slot, source, over_tokens, preferred_element_type=F32
+        ).astype(BF16)
+        for e in range(n_lang):
+            slots[e, k] = packed[e * cap:(e + 1) * cap]
+
+    started = []
+
+    def copy(kind, k, j, src, dst, dev):
+        return pltpu.make_async_remote_copy(
+            src_ref=src, dst_ref=dst, send_sem=send_sem.at[kind, k, j],
+            recv_sem=recv_sem.at[kind, k, j], device_id=dev, device_id_type=MESH,
+        )
+
+    def send(kind, k, j, src, dst, dev):
+        going = copy(kind, k, j, src, dst, dev)
+        going.start()
+        started.append(going)
+
+    def recv(kind, k, j, dst, dev):
+        copy(kind, k, j, dst, dst, dev).wait_recv()
+
+    def piece(k, f, j, row_y, part=None):
+        first = j * block + row_y * cap
+        size = cap
+        if part is not None:
+            first = first + part * half
+            size = half
+        return rows.at[k, f, pl.ds(pl.multiple_of(first, half), size)]
+
+    pl.semaphore_wait(barrier, len(others))
+    for k in range(2):
+        for j in range(1, n_lang):
+            send(ZOUT, k, j, slots.at[plane[j], k], piece(k, ti, j, y), z_dev[j])
+    for k in range(2):
+        piece(k, ti, 0, y)[...] = slots[z, k]
+
+    def g0(q):
+        k, j = q // n_lang, q % n_lang
+        own = piece(k, ti, j, y)
+        if j:
+            recv(ZOUT, k, j, own, z_dev[j])
+        send(XOWN, k, j, own, own, x_dev)
+        send(YOWN, k, j, own, own, y_dev)
+        send(SOWN, k, j, own, own, s_dev)
+
+    def g1(q):
+        k, j = q // n_lang, q % n_lang
+        from_x, from_y = piece(k, tix, j, y), piece(k, ti, j, ny)
+        recv(XOWN, k, j, from_x, x_dev)
+        part = piece(k, tix, j, y, 0)
+        send(FWDA, k, j, part, part, y_dev)
+        send(SPX, k, j, from_x, from_x, s_dev)
+        recv(YOWN, k, j, from_y, y_dev)
+        part = piece(k, ti, j, ny, 1)
+        send(FWDB, k, j, part, part, x_dev)
+        send(SPY, k, j, from_y, from_y, s_dev)
+
+    def g2(q):
+        k, j = q // n_lang, q % n_lang
+        recv(FWDA, k, j, piece(k, tix, j, ny, 0), y_dev)
+        recv(FWDB, k, j, piece(k, tix, j, ny, 1), x_dev)
+        diag = piece(k, tix, j, ny)
+        send(SPD, k, j, diag, diag, s_dev)
+
+    def g3(q):
+        k, j = q // n_lang, q % n_lang
+        recv(SOWN, k, j, piece(k, tis, j, y), s_dev)
+        recv(SPX, k, j, piece(k, tixs, j, y), s_dev)
+        recv(SPY, k, j, piece(k, tis, j, ny), s_dev)
+        recv(SPD, k, j, piece(k, tixs, j, ny), s_dev)
+
+    size = 2 * block
+    n_feat = rows.shape[1]
+    over_cols = (((1,), (1,)), ((), ()))
+
+    def all_feats(k, g):
+        return jnp.concatenate(
+            [rows[k, f, g * size:(g + 1) * size] for f in range(n_feat)], axis=1
+        )
+
+    def forward(g):
+        at = slice(g * size, (g + 1) * size)
+        here = all_feats(0, g)
+        gp = jnp.dot(here, wg[...], preferred_element_type=F32)
+        up = jnp.dot(here, wu[...], preferred_element_type=F32)
+        gate_pre[at] = gp
+        up_pre[at] = up
+        hidden[at] = (gp * jax.nn.sigmoid(gp) * up).astype(BF16)
+
+    def backward(g):
+        at = slice(g * size, (g + 1) * size)
+        gh = lax.dot_general(all_feats(1, g), wd[...], over_cols, preferred_element_type=F32)
+        gp, up = gate_pre[at], up_pre[at]
+        s = jax.nn.sigmoid(gp)
+        ggp[at] = (gh * up * s * (1.0 + gp * (1.0 - s))).astype(BF16)
+        gup[at] = (gh * (gp * s)).astype(BF16)
+
+    def sums(k, g):
+        at = slice(g * size, (g + 1) * size)
+
+        def one(f):
+            feats = pl.ds(pl.multiple_of(f * width, width), width)
+            if k == 0:
+                return jnp.dot(hidden[at], wd[:, feats], preferred_element_type=F32)
+            return lax.dot_general(
+                ggp[at], wg[feats, :], over_cols, preferred_element_type=F32
+            ) + lax.dot_general(gup[at], wu[feats, :], over_cols, preferred_element_type=F32)
+
+        for ax in range(2):
+            sib_src[k, ax, at] = one(ax * 2 + 1 - c).astype(BF16)
+        for j in (2 * g, 2 * g + 1):
+            part = pl.ds(j * block, block)
+            send(RSIB, k, j, sib_src.at[k, :, part], sib_dst.at[k, :, part], s_dev)
+        for ax in range(2):
+            keep[k, ax, at] = one(ax * 2 + c)
+
+    def pair_sum(k, j, at_x, at_y):
+        where = pl.ds(pl.multiple_of(j * block + at_y * cap, cap), cap)
+        return keep[k, at_x, where] + sib_dst[k, at_x, where].astype(F32)
+
+    def r1(q):
+        k, j = q // n_lang, q % n_lang
+        part = pl.ds(j * block, block)
+        recv(RSIB, k, j, sib_dst.at[k, :, part], s_dev)
+        diag_src[k, j] = pair_sum(k, j, nx, ny).astype(BF16)
+        top, low = pl.ds(0, half), pl.ds(half, half)
+        send(RDA, k, j, diag_src.at[k, j, top], diag_dst.at[k, j, top], y_dev)
+        send(RDB, k, j, diag_src.at[k, j, low], diag_dst.at[k, j, low], x_dev)
+
+    def r2(q):
+        k, j = q // n_lang, q % n_lang
+        top, low = pl.ds(0, half), pl.ds(half, half)
+        recv(RDA, k, j, diag_dst.at[k, j, top], y_dev)
+        to_x = pair_sum(k, j, nx, y)
+        nx_src[k, j, top] = (to_x[:half] + diag_dst[k, j, top].astype(F32)).astype(BF16)
+        nx_src[k, j, low] = to_x[half:].astype(BF16)
+        send(RX, k, j, nx_src.at[k, j], nx_dst.at[k, j], x_dev)
+        recv(RDB, k, j, diag_dst.at[k, j, low], x_dev)
+        to_y = pair_sum(k, j, x, ny)
+        ny_src[k, j, top] = to_y[:half].astype(BF16)
+        ny_src[k, j, low] = (to_y[half:] + diag_dst[k, j, low].astype(F32)).astype(BF16)
+        send(RY, k, j, ny_src.at[k, j], ny_dst.at[k, j], y_dev)
+
+    def r3(q):
+        k, j = q // n_lang, q % n_lang
+        recv(RX, k, j, nx_dst.at[k, j], x_dev)
+        recv(RY, k, j, ny_dst.at[k, j], y_dev)
+        total = pair_sum(k, j, x, y) + nx_dst[k, j].astype(F32) + ny_dst[k, j].astype(F32)
+        if j:
+            back_src[k, j] = total.astype(BF16)
+            send(RZ, k, j, back_src.at[k, j], back.at[k, z], z_dev[j])
+        else:
+            back[k, z] = total.astype(BF16)
+
+    def home(k, out_ref):
+        for j in range(1, n_lang):
+            recv(RZ, k, j, back.at[k, plane[j]], z_dev[j])
+        flat = back[k].reshape(n_lang * cap, width)
+        out_ref[...] = jnp.dot(to_slot, flat, preferred_element_type=F32).astype(BF16)
+
+    stores = []
+
+    def store(src, dst, n):
+        going = pltpu.make_async_copy(src, dst, local_sem.at[n])
+        going.start()
+        stores.append(going)
+
+    g0(0)
+    g0(1), g1(0)
+    g0(2), g1(1), g2(0)
+    g0(3), g1(2), g2(1), g3(0)
+    g0(4), g1(3), g2(2), g3(1)
+    for load in loads:
+        load.wait()
+    forward(0)
+    g0(5), g1(4), g2(3), g3(2)
+    g0(6), g1(5), g2(4), g3(3)
+    forward(1)
+    g0(7), g1(6), g2(5), g3(4)
+    sums(0, 0)
+    g1(7), g2(6), g3(5)
+    r1(0), r1(1)
+    backward(0)
+    g2(7), g3(6)
+    sums(0, 1)
+    g3(7)
+    r2(0), r2(1), r1(2), r1(3)
+    backward(1)
+    store(rows, rows_hbm, 3)
+    store(hidden, hid_hbm, 4)
+    store(ggp, ggp_hbm, 5)
+    store(gup, gup_hbm, 6)
+    r3(0), r3(1), r2(2), r2(3)
+    sums(1, 0)
+    r3(2), r3(3), r1(4), r1(5)
+    sums(1, 1)
+    r2(4), r2(5), r1(6), r1(7)
+    r3(4), r3(5), r2(6), r2(7)
+    home(0, y_ref)
+    r3(6), r3(7)
+    home(1, yg_ref)
+    for going in started:
+        going.wait_send()
+    for going in stores:
+        going.wait()
+
+
+def weight_grad_kernel(rows_ref, grads_ref, hid_ref, ggp_ref, gup_ref, dg_ref, du_ref, dd_ref):
+    over_rows = (((0,), (0,)), ((), ()))
+    here = rows_ref[0, 0]
+    dg_ref[0] = lax.dot_general(here, ggp_ref[...], over_rows, preferred_element_type=F32).astype(BF16)
+    du_ref[0] = lax.dot_general(here, gup_ref[...], over_rows, preferred_element_type=F32).astype(BF16)
+    dd_ref[0] = lax.dot_general(
+        hid_ref[...], grads_ref[0, 0], over_rows, preferred_element_type=F32
+    ).astype(BF16)
+
+
+def fused_body(
+    tokens, labels, domain_ids, domain_weights, cotangent, gate_weight, up_weight, down_weight
+):
+    n_lang = lax.axis_size("expert") // SPLIT
+    n_feat = lax.axis_size("tensor")
+    n_tok, width = tokens.shape
+    cap = 2 * n_tok // n_lang
+    n_rows = n_lang * SPLIT * cap
+    feats = n_feat * width
+    hid = gate_weight.shape[2]
+    vmem = pl.BlockSpec(memory_space=pltpu.VMEM)
+    hbm = pl.BlockSpec(memory_space=pl.ANY)
+    out = jax.ShapeDtypeStruct((n_tok, width), BF16)
+    act = jax.ShapeDtypeStruct((n_rows, hid), BF16)
+    slab = pltpu.VMEM((2, n_lang, cap, width), BF16)
+    y, yg, rows, hidden, ggp, gup = pl.pallas_call(
+        expert_kernel,
+        out_shape=(
+            out, out, jax.ShapeDtypeStruct((2, n_feat, n_rows, width), BF16), act, act, act
+        ),
+        in_specs=[vmem] * 5 + [hbm] * 3,
+        out_specs=(vmem, vmem, hbm, hbm, hbm, hbm),
+        scratch_shapes=[
+            pltpu.VMEM((feats, hid), BF16),
+            pltpu.VMEM((feats, hid), BF16),
+            pltpu.VMEM((hid, feats), BF16),
+            pltpu.VMEM((n_lang, 2, cap, width), BF16),
+            pltpu.VMEM((2, n_feat, n_rows, width), BF16),
+            pltpu.VMEM((n_rows, hid), F32),
+            pltpu.VMEM((n_rows, hid), F32),
+            pltpu.VMEM((n_rows, hid), BF16),
+            pltpu.VMEM((n_rows, hid), BF16),
+            pltpu.VMEM((n_rows, hid), BF16),
+            pltpu.VMEM((2, 2, n_rows, width), F32),
+            pltpu.VMEM((2, 2, n_rows, width), BF16),
+            pltpu.VMEM((2, 2, n_rows, width), BF16),
+            slab, slab, slab, slab, slab, slab, slab, slab,
+            pltpu.SemaphoreType.DMA((KINDS, 2, n_lang)),
+            pltpu.SemaphoreType.DMA((KINDS, 2, n_lang)),
+            pltpu.SemaphoreType.DMA((7,)),
+        ],
+        compiler_params=pltpu.CompilerParams(
+            collective_id=0, has_side_effects=True, vmem_limit_bytes=48 * 2**20
+        ),
+        name="expert_layer",
+    )(
+        tokens, cotangent, labels, domain_ids.reshape(1, n_tok),
+        domain_weights.reshape(1, -1), gate_weight, up_weight, down_weight,
+    )
+    whole_act = pl.BlockSpec((n_rows, hid), lambda f: (0, 0))
+    dg, du, dd = pl.pallas_call(
+        weight_grad_kernel,
+        grid=(n_feat,),
+        out_shape=(
+            jax.ShapeDtypeStruct(gate_weight.shape, BF16),
+            jax.ShapeDtypeStruct(up_weight.shape, BF16),
+            jax.ShapeDtypeStruct(down_weight.shape, BF16),
+        ),
+        in_specs=[
+            pl.BlockSpec((1, 1, n_rows, width), lambda f: (0, f, 0, 0)),
+            pl.BlockSpec((1, 1, n_rows, width), lambda f: (1, f, 0, 0)),
+            whole_act, whole_act, whole_act,
+        ],
+        out_specs=(
+            pl.BlockSpec((1, width, hid), lambda f: (0, f, 0)),
+            pl.BlockSpec((1, width, hid), lambda f: (0, f, 0)),
+            pl.BlockSpec((1, hid, width), lambda f: (0, 0, f)),
+        ),
+        compiler_params=pltpu.CompilerParams(vmem_limit_bytes=32 * 2**20),
+        name="weight_grads",
+    )(rows, rows, hidden, ggp, gup)
+    return (y, yg, dg, du, dd)
+
+
 def solution(mesh):
+    n_lang = mesh.shape["expert"] // SPLIT
+    fits = n_lang == 4 and mesh.shape["tensor"] == 4
     return jax.shard_map(
-        body,
+        fused_body if fits else body,
         mesh=mesh,
         in_specs=(
             P("expert", "tensor"),

time: 290 us -> 76.3 us (0.26)
  waiting for transfers between devices: 131 us -> 0 us
  blocking collectives: 98.8 us -> 0 us
  Pallas kernels: 0 us -> 66.5 us
  matrix products: 27.2 us -> 0 us
  between operations: 14 us -> 0.66 us
  starting transfers between devices: 7.15 us -> 0 us
  other arithmetic: 5.78 us -> 0 us
  local copies, waits for them, and re-layouts: 5.37 us -> 8.96 us
    all_to_all x1 -> x0, blocking collectives: 98.8 us -> none  [body(): lax.all_to_all(outbound, 'expert', split_axis=1, concat_axis=1, tiled=True)]
    reduce_scatter x2 -> x0, waiting for transfers between devices: 85.1 us -> none  [the longest x1 47.2 us: body(): lax.psum_scatter(out_part, 'tensor', scatter_dimension=2, tiled=True)]
    pallas_call x0 -> x2, Pallas kernels: none -> 66.5 us  [the longest x1 61.5 us: fused_body(): pl.pallas_call(expert_kernel, out_shape=(out, out, jax.ShapeDtypeStruct((...]
    dot_general x12 -> x0, matrix products: 27.2 us -> none  [the longest x1 4.84 us: body(): out_part = jnp.dot(hidden, w_down, preferred_element_type=jnp.float32)]
    ppermute x1 -> x0, waiting for transfers between devices: 23.4 us -> none  [partner(): lax.ppermute(value, axis, [(i, i ^ 1 << stride) for i in range(lax.axis_s...]
    all_gather x1 -> x0, waiting for transfers between devices: 18.7 us -> none  [body(): sources = lax.all_gather(sources, 'tensor', axis=2, tiled=True)]
    unnamed x32 -> x15, local copies, waits for them, and re-layouts: 3.39 us -> 8.96 us
    all_to_all x1 -> x0, starting transfers between devices: 5.5 us -> none  [body(): lax.all_to_all(going_back, 'expert', split_axis=1, concat_axis=1, tiled=T...]
  transfers between devices with their start and end apart: 5 -> 0, of which waited for: 5 -> 0; matrix products, arithmetic and copies ran while one was open for 5% -> 0% of each run, Pallas kernels for 0% -> 0%
where the time goes in v1:
time: 76.3 us; the launch traced here: 76.1 us
  Pallas kernels  66.5 us (87%)
  local copies, waits for them, and re-layouts  8.96 us (12%)
    pallas_call x1, Pallas kernels, fused_body(): pl.pallas_call(expert_kernel, out_shape=(out, out, jax.ShapeDtypeStruct((...  61.5 us
    unnamed x15, local copies, waits for them, and re-layouts  8.96 us
    pallas_call x1, Pallas kernels, fused_body(): pl.pallas_call(weight_grad_kernel, grid=(n_feat,), out_shape=(jax.ShapeDt...  4.92 us

profile of v1, /device:TPU:0, one launch (start us, length us, event | category | flops | bytes accessed | tf_op | source)
XLA Modules:
  0.0 76.1 jit_solution(9390116858448083981)
XLA Ops:
  0.6 0.8 %copy.13.lab_ref = s32[128,1]{1,0:T(8,128)S(1)} copy(s32[128,1]{0,1:T(1,128)} %param.9) | data formatting | bytes 1024 | tf_op args[1]
  1.4 0.0 copy-start.1
  1.4 1.6 %copy-done.1 = bf16[1,2048,512]{2,1,0:T(8,128)(2,1)S(1)} copy-done((bf16[1,2048,512]{2,1,0:T(8,128)(2,1)S(1)}, bf16[1,2048,512]{2,1,0:T(8,128)(2,1)}, u32[]{:S(2)}) %copy-start.1) | copy-done | bytes 2097176
  3.0 0.0 copy-start.2
  3.0 0.9 %copy-done.2 = bf16[128,512]{1,0:T(8,128)(2,1)S(1)} copy-done((bf16[128,512]{1,0:T(8,128)(2,1)S(1)}, bf16[128,512]{1,0:T(8,128)(2,1)}, u32[]{:S(2)}) %copy-start.2) | copy-done | bytes 131096
  3.9 0.0 copy-start.3
  3.9 0.9 %copy-done.3 = bf16[128,512]{1,0:T(8,128)(2,1)S(1)} copy-done((bf16[128,512]{1,0:T(8,128)(2,1)S(1)}, bf16[128,512]{1,0:T(8,128)(2,1)}, u32[]{:S(2)}) %copy-start.3) | copy-done | bytes 131096
  4.8 0.0 copy-start.4
  4.8 0.7 copy-done.4
  5.5 0.0 copy-start.5
  5.5 0.7 copy-done.5
  6.1 61.5 %expert_layer.1 = (bf16[128,512]{1,0:T(8,128)(2,1)S(1)}, bf16[128,512]{1,0:T(8,128)(2,1)S(1)}, bf16[2,4,512,512]{3,2,1,0:T(8,128)(2,1)}, bf16[512,512]{1,0:T(8,1...) custom-call(bf16[128,512]{1,0:T(8,128)(2,1)S(1)} %copy-done.2, bf16[128,512]{1,0:T(8,128)(2,1)S(1)} %copy-done.3, ...), custom_call_target="tpu_custom_call" | custom-call | tf_op jit(solution)/shard_map/expert_layer/pallas_call | solution.py:404
  67.7 0.0 copy-start
  67.7 2.2 %copy-done = bf16[2,4,512,512]{3,2,1,0:T(8,128)(2,1)S(1)} copy-done((bf16[2,4,512,512]{3,2,1,0:T(8,128)(2,1)S(1)}, bf16[2,4,512,512]{3,2,1,0:T(8,128)(2,1)}, u32[]{:S(2)}) %copy-start) | copy-done | bytes 4194328
  69.8 4.9 %weight_grads.1 = (bf16[1,2048,512]{2,1,0:T(8,128)(2,1)}, bf16[1,2048,512]{2,1,0:T(8,128)(2,1)}, bf16[1,512,2048]{2,1,0:T(8,128)(2,1)}) custom-call(bf16[2,4,512,512]{3,2,1,0:T(8,128)(2,1)S(1)} %copy-done, bf16[2,4,512,512]{3,2,1,0:T(8,128)(2,1)S(1)} %copy-done, bf16[512,512]{1,0:T(8,128)(2,1)S(1)} %get-tuple-element.17.hid_ref, ...), custom_call_target="tpu_custom_call" | custom-call | tf_op jit(solution)/shard_map/weight_grads/pallas_call | solution.py:439
  74.8 0.7 copy.16
  75.4 0.7 copy.17
Async XLA Ops:
  1.4 1.6 %copy-start.1 = (bf16[1,2048,512]{2,1,0:T(8,128)(2,1)S(1)}, bf16[1,2048,512]{2,1,0:T(8,128)(2,1)}, u32[]{:S(2)}) copy-start(bf16[1,2048,512]{2,1,0:T(8,128)(2,1)} %wg_hbm.1) | copy-start | bytes 6291460
  3.0 0.9 %copy-start.2 = (bf16[128,512]{1,0:T(8,128)(2,1)S(1)}, bf16[128,512]{1,0:T(8,128)(2,1)}, u32[]{:S(2)}) copy-start(bf16[128,512]{1,0:T(8,128)(2,1)} %tok_ref.1) | copy-start | bytes 393220
  3.9 0.9 %copy-start.3 = (bf16[128,512]{1,0:T(8,128)(2,1)S(1)}, bf16[128,512]{1,0:T(8,128)(2,1)}, u32[]{:S(2)}) copy-start(bf16[128,512]{1,0:T(8,128)(2,1)} %cot_ref.1) | copy-start | bytes 393220
  4.8 0.7 copy-start.4
  5.5 0.7 copy-start.5
  67.7 2.2 %copy-start = (bf16[2,4,512,512]{3,2,1,0:T(8,128)(2,1)S(1)}, bf16[2,4,512,512]{3,2,1,0:T(8,128)(2,1)}, u32[]{:S(2)}) copy-start(bf16[2,4,512,512]{3,2,1,0:T(8,128)(2,1)} %get-tuple-element.16.rows_ref.grads_ref) | copy-start | bytes 12582916

commit v2 on v1

--- a/solution.py
+++ b/solution.py
@@ -114,11 +114,11 @@
 
 
 def expert_kernel(
-    tok_ref, cot_ref, lab_ref, dom_ref, dw_ref, wg_hbm, wu_hbm, wd_hbm,
-    y_ref, yg_ref, rows_hbm, hid_hbm, ggp_hbm, gup_hbm,
-    wg, wu, wd, slots, rows, gate_pre, up_pre, hidden, ggp, gup, keep,
+    tok_hbm, cot_hbm, lab_hbm, dom_hbm, dw_hbm, wg_hbm, wu_hbm, wd_hbm,
+    map_hbm, back_hbm, dg_hbm, du_hbm, dd_hbm,
+    slot_map, back, dg, du, dd, tok_ref, cot_ref, lab_ref, dom_ref, dw_ref, wg, wu, wd, slots, rows, gate_pre, up_pre, hidden, ggp, gup, keep,
     sib_src, sib_dst, diag_src, diag_dst, nx_src, nx_dst, ny_src, ny_dst,
-    back_src, back, send_sem, recv_sem, local_sem,
+    back_src, send_sem, recv_sem, local_sem,
 ):
     n_tok, width = tok_ref.shape
     n_lang = slots.shape[0]
@@ -138,9 +138,11 @@
     z_dev = [(plane[j] * 2 + y, ti) for j in range(n_lang)]
 
     loads = [
-        pltpu.make_async_copy(wg_hbm.at[0], wg, local_sem.at[0]),
-        pltpu.make_async_copy(wu_hbm.at[0], wu, local_sem.at[1]),
-        pltpu.make_async_copy(wd_hbm.at[0], wd, local_sem.at[2]),
+        pltpu.make_async_copy(src, dst, local_sem.at[n])
+        for n, (src, dst) in enumerate((
+            (lab_hbm, lab_ref), (tok_hbm, tok_ref), (dom_hbm, dom_ref), (dw_hbm, dw_ref),
+            (cot_hbm, cot_ref), (wg_hbm.at[0], wg), (wu_hbm.at[0], wu), (wd_hbm.at[0], wd),
+        ))
     ]
     barrier = pltpu.get_barrier_semaphore()
     others = [x_dev, y_dev, s_dev] + z_dev[1:]
@@ -149,31 +151,6 @@
     for copy in loads:
         copy.start()
 
-    lab = lab_ref[...]
-    lane = lax.broadcasted_iota(jnp.int32, (n_tok, n_tok), 1)
-    sub = lax.broadcasted_iota(jnp.int32, (n_tok, n_tok), 0)
-    lab_hot = jnp.where(lane == lab, 1.0, 0.0)
-    earlier = jnp.where(lane < sub, 1.0, 0.0).astype(BF16)
-    before = jnp.dot(earlier, lab_hot.astype(BF16), preferred_element_type=F32)
-    pos = jnp.sum(before * lab_hot, axis=1, keepdims=True)
-    target = lab.astype(F32) * cap + pos
-    slot_lane = lax.broadcasted_iota(jnp.int32, (n_tok, n_lang * cap), 1).astype(F32)
-    to_slot = jnp.where(slot_lane == target, 1.0, 0.0).astype(BF16)
-    dom_row = jnp.broadcast_to(dom_ref[...].astype(F32), (n_tok, n_tok))
-    dom_col = jnp.sum(jnp.where(lane == sub, dom_row, 0.0), axis=1, keepdims=True)
-    n_dom = dw_ref.shape[1]
-    dom_lane = lax.broadcasted_iota(jnp.int32, (n_tok, n_dom), 1).astype(F32)
-    dw_row = jnp.broadcast_to(dw_ref[...], (n_tok, n_dom))
-    scale = jnp.sum(jnp.where(dom_lane == dom_col, dw_row, 0.0), axis=1, keepdims=True)
-    grad_rows = (scale * cot_ref[...].astype(F32)).astype(BF16)
-    over_tokens = (((0,), (0,)), ((), ()))
-    for k, source in enumerate((tok_ref[...], grad_rows)):
-        packed = lax.dot_general(
-            to_slot, source, over_tokens, preferred_element_type=F32
-        ).astype(BF16)
-        for e in range(n_lang):
-            slots[e, k] = packed[e * cap:(e + 1) * cap]
-
     started = []
 
     def copy(kind, k, j, src, dst, dev):
@@ -198,15 +175,56 @@
             size = half
         return rows.at[k, f, pl.ds(pl.multiple_of(first, half), size)]
 
-    pl.semaphore_wait(barrier, len(others))
-    for k in range(2):
+    loads[0].wait()
+    lane = lax.broadcasted_iota(jnp.int32, (n_tok, n_tok), 1)
+    sub = lax.broadcasted_iota(jnp.int32, (n_tok, n_tok), 0)
+
+    def column(row_ref):
+        wide = jnp.broadcast_to(row_ref[...].astype(F32), (n_tok, n_tok))
+        return jnp.sum(jnp.where(lane == sub, wide, 0.0), axis=1, keepdims=True)
+
+    lab = column(lab_ref)
+    lab_hot = jnp.where(lane.astype(F32) == lab, 1.0, 0.0)
+    earlier = jnp.where(lane < sub, 1.0, 0.0).astype(BF16)
+    before = jnp.dot(earlier, lab_hot.astype(BF16), preferred_element_type=F32)
+    pos = jnp.sum(before * lab_hot, axis=1, keepdims=True)
+    target = lab * cap + pos
+    slot_lane = lax.broadcasted_iota(jnp.int32, (n_tok, n_lang * cap), 1).astype(F32)
+    to_slot = jnp.where(slot_lane == target, 1.0, 0.0).astype(BF16)
+    slot_map[...] = to_slot
+    map_store = pltpu.make_async_copy(slot_map, map_hbm, local_sem.at[21])
+    map_store.start()
+    over_tokens = (((0,), (0,)), ((), ()))
+
+    def pack(k, source):
+        packed = lax.dot_general(
+            to_slot, source, over_tokens, preferred_element_type=F32
+        ).astype(BF16)
+        for e in range(n_lang):
+            slots[e, k] = packed[e * cap:(e + 1) * cap]
+
+    def exchange(k):
         for j in range(1, n_lang):
             send(ZOUT, k, j, slots.at[plane[j], k], piece(k, ti, j, y), z_dev[j])
-    for k in range(2):
         piece(k, ti, 0, y)[...] = slots[z, k]
 
+    loads[1].wait()
+    pack(0, tok_ref[...])
+    pl.semaphore_wait(barrier, len(others))
+    exchange(0)
+    for load in loads[2:5]:
+        load.wait()
+    n_dom = dw_ref.shape[1]
+    dom_lane = lax.broadcasted_iota(jnp.int32, (n_tok, n_dom), 1).astype(F32)
+    dw_row = jnp.broadcast_to(dw_ref[...], (n_tok, n_dom))
+    scale = jnp.sum(
+        jnp.where(dom_lane == column(dom_ref), dw_row, 0.0), axis=1, keepdims=True
+    )
+
+    order = [(0, 0), (1, 0), (0, 1), (0, 2), (0, 3), (1, 1), (1, 2), (1, 3)]
+
     def g0(q):
-        k, j = q // n_lang, q % n_lang
+        k, j = order[q]
         own = piece(k, ti, j, y)
         if j:
             recv(ZOUT, k, j, own, z_dev[j])
@@ -215,7 +233,7 @@
         send(SOWN, k, j, own, own, s_dev)
 
     def g1(q):
-        k, j = q // n_lang, q % n_lang
+        k, j = order[q]
         from_x, from_y = piece(k, tix, j, y), piece(k, ti, j, ny)
         recv(XOWN, k, j, from_x, x_dev)
         part = piece(k, tix, j, y, 0)
@@ -227,14 +245,14 @@
         send(SPY, k, j, from_y, from_y, s_dev)
 
     def g2(q):
-        k, j = q // n_lang, q % n_lang
+        k, j = order[q]
         recv(FWDA, k, j, piece(k, tix, j, ny, 0), y_dev)
         recv(FWDB, k, j, piece(k, tix, j, ny, 1), x_dev)
         diag = piece(k, tix, j, ny)
         send(SPD, k, j, diag, diag, s_dev)
 
     def g3(q):
-        k, j = q // n_lang, q % n_lang
+        k, j = order[q]
         recv(SOWN, k, j, piece(k, tis, j, y), s_dev)
         recv(SPX, k, j, piece(k, tixs, j, y), s_dev)
         recv(SPY, k, j, piece(k, tis, j, ny), s_dev)
@@ -323,67 +341,105 @@
         else:
             back[k, z] = total.astype(BF16)
 
-    def home(k, out_ref):
-        for j in range(1, n_lang):
-            recv(RZ, k, j, back.at[k, plane[j]], z_dev[j])
-        flat = back[k].reshape(n_lang * cap, width)
-        out_ref[...] = jnp.dot(to_slot, flat, preferred_element_type=F32).astype(BF16)
+    over_rows = (((0,), (0,)), ((), ()))
 
     stores = []
 
-    def store(src, dst, n):
-        going = pltpu.make_async_copy(src, dst, local_sem.at[n])
+    def store(src, dst):
+        going = pltpu.make_async_copy(src, dst, local_sem.at[8 + len(stores)])
         going.start()
         stores.append(going)
 
+    def weight_grad(which, f):
+        at = slice(f * width, (f + 1) * width)
+        if which == 2:
+            dd[0, :, at] = lax.dot_general(
+                hidden[...], rows[1, f], over_rows, preferred_element_type=F32
+            ).astype(BF16)
+            store(dd.at[0, :, at], dd_hbm.at[0, :, at])
+        else:
+            out, grad, out_hbm = ((dg, ggp, dg_hbm), (du, gup, du_hbm))[which]
+            out[0, at] = lax.dot_general(
+                rows[0, f], grad[...], over_rows, preferred_element_type=F32
+            ).astype(BF16)
+            store(out.at[0, at], out_hbm.at[0, at])
+
     g0(0)
+    pack(1, (scale * cot_ref[...].astype(F32)).astype(BF16))
+    exchange(1)
     g0(1), g1(0)
     g0(2), g1(1), g2(0)
     g0(3), g1(2), g2(1), g3(0)
     g0(4), g1(3), g2(2), g3(1)
-    for load in loads:
+    for load in loads[5:]:
         load.wait()
+    g0(5), g1(4), g2(3), g3(2)
+    g0(6)
     forward(0)
-    g0(5), g1(4), g2(3), g3(2)
-    g0(6), g1(5), g2(4), g3(3)
+    g1(5), g2(4), g3(3), g0(7)
+    sums(0, 0)
+    g1(6), g2(5), g3(4), r1(0)
     forward(1)
-    g0(7), g1(6), g2(5), g3(4)
-    sums(0, 0)
-    g1(7), g2(6), g3(5)
-    r1(0), r1(1)
+    g1(7), g2(6), g3(5), r1(1)
     backward(0)
-    g2(7), g3(6)
+    r2(0), r2(1)
     sums(0, 1)
-    g3(7)
-    r2(0), r2(1), r1(2), r1(3)
+    g2(7), g3(6), g3(7), r1(2), r1(3)
+    sums(1, 0)
+    r3(0), r3(1), r2(2), r2(3), r1(4), r1(5)
     backward(1)
-    store(rows, rows_hbm, 3)
-    store(hidden, hid_hbm, 4)
-    store(ggp, ggp_hbm, 5)
-    store(gup, gup_hbm, 6)
-    r3(0), r3(1), r2(2), r2(3)
-    sums(1, 0)
-    r3(2), r3(3), r1(4), r1(5)
+    r3(2), r3(3), r2(4), r2(5)
     sums(1, 1)
-    r2(4), r2(5), r1(6), r1(7)
-    r3(4), r3(5), r2(6), r2(7)
-    home(0, y_ref)
+    r1(6), r1(7), r3(4), r3(5)
+    weight_grad(2, 0), weight_grad(2, 1)
+    r2(6), r2(7)
+    for f in range(2, n_feat):
+        weight_grad(2, f)
+    weight_grad(0, 0)
     r3(6), r3(7)
-    home(1, yg_ref)
+    for f in range(1, n_feat):
+        weight_grad(0, f)
+    for f in range(n_feat):
+        weight_grad(1, f)
+    for k in range(2):
+        for j in range(1, n_lang):
+            recv(RZ, k, j, back.at[k, plane[j]], z_dev[j])
+    store(back, back_hbm)
     for going in started:
         going.wait_send()
-    for going in stores:
+    for going in stores + [map_store]:
         going.wait()
 
 
-def weight_grad_kernel(rows_ref, grads_ref, hid_ref, ggp_ref, gup_ref, dg_ref, du_ref, dd_ref):
-    over_rows = (((0,), (0,)), ((), ()))
-    here = rows_ref[0, 0]
-    dg_ref[0] = lax.dot_general(here, ggp_ref[...], over_rows, preferred_element_type=F32).astype(BF16)
-    du_ref[0] = lax.dot_general(here, gup_ref[...], over_rows, preferred_element_type=F32).astype(BF16)
-    dd_ref[0] = lax.dot_general(
-        hid_ref[...], grads_ref[0, 0], over_rows, preferred_element_type=F32
-    ).astype(BF16)
+def home_kernel(
+    map_hbm, back_hbm, dg_in, du_in, dd_in, y_ref, yg_ref, dg_out, du_out, dd_out,
+    slot_map, back, dg, du, dd, sem,
+):
+    first = [
+        pltpu.make_async_copy(map_hbm, slot_map, sem.at[0]),
+        pltpu.make_async_copy(back_hbm, back, sem.at[1]),
+    ]
+    into, outof = [], []
+    for src, held, dst in ((dg_in, dg, dg_out), (du_in, du, du_out), (dd_in, dd, dd_out)):
+        step = src.shape[1] // 4
+        for n in range(4):
+            part = pl.ds(n * step, step)
+            at = 2 + 2 * len(into)
+            into.append(pltpu.make_async_copy(src.at[0, part], held.at[0, part], sem.at[at]))
+            outof.append(pltpu.make_async_copy(held.at[0, part], dst.at[0, part], sem.at[at + 1]))
+    for going in first + into:
+        going.start()
+    for going in first:
+        going.wait()
+    _, n_lang, cap, width = back.shape
+    for k, out_ref in enumerate((y_ref, yg_ref)):
+        flat = back[k].reshape(n_lang * cap, width)
+        out_ref[...] = jnp.dot(slot_map[...], flat, preferred_element_type=F32).astype(BF16)
+    for arriving, leaving in zip(into, outof):
+        arriving.wait()
+        leaving.start()
+    for going in outof:
+        going.wait()
 
 
 def fused_body(
@@ -397,18 +453,31 @@
     feats = n_feat * width
     hid = gate_weight.shape[2]
     vmem = pl.BlockSpec(memory_space=pltpu.VMEM)
-    hbm = pl.BlockSpec(memory_space=pl.ANY)
+    hbm = pl.BlockSpec(memory_space=pltpu.HBM)
     out = jax.ShapeDtypeStruct((n_tok, width), BF16)
-    act = jax.ShapeDtypeStruct((n_rows, hid), BF16)
     slab = pltpu.VMEM((2, n_lang, cap, width), BF16)
-    y, yg, rows, hidden, ggp, gup = pl.pallas_call(
+    grads = tuple(
+        jax.ShapeDtypeStruct(w.shape, BF16) for w in (gate_weight, up_weight, down_weight)
+    )
+    parts = pl.pallas_call(
         expert_kernel,
         out_shape=(
-            out, out, jax.ShapeDtypeStruct((2, n_feat, n_rows, width), BF16), act, act, act
-        ),
-        in_specs=[vmem] * 5 + [hbm] * 3,
-        out_specs=(vmem, vmem, hbm, hbm, hbm, hbm),
+            jax.ShapeDtypeStruct((n_tok, n_lang * cap), BF16),
+            jax.ShapeDtypeStruct((2, n_lang, cap, width), BF16),
+        ) + grads,
+        in_specs=[hbm] * 8,
+        out_specs=(hbm,) * 5,
         scratch_shapes=[
+            pltpu.VMEM((n_tok, n_lang * cap), BF16),
+            slab,
+            pltpu.VMEM(gate_weight.shape, BF16),
+            pltpu.VMEM(up_weight.shape, BF16),
+            pltpu.VMEM(down_weight.shape, BF16),
+            pltpu.VMEM((n_tok, width), BF16),
+            pltpu.VMEM((n_tok, width), BF16),
+            pltpu.VMEM((1, n_tok), jnp.int32),
+            pltpu.VMEM((1, n_tok), jnp.int32),
+            pltpu.VMEM((1, domain_weights.shape[0]), F32),
             pltpu.VMEM((feats, hid), BF16),
             pltpu.VMEM((feats, hid), BF16),
             pltpu.VMEM((hid, feats), BF16),
@@ -422,42 +491,35 @@
             pltpu.VMEM((2, 2, n_rows, width), F32),
             pltpu.VMEM((2, 2, n_rows, width), BF16),
             pltpu.VMEM((2, 2, n_rows, width), BF16),
-            slab, slab, slab, slab, slab, slab, slab, slab,
+            slab, slab, slab, slab, slab, slab, slab,
             pltpu.SemaphoreType.DMA((KINDS, 2, n_lang)),
             pltpu.SemaphoreType.DMA((KINDS, 2, n_lang)),
-            pltpu.SemaphoreType.DMA((7,)),
+            pltpu.SemaphoreType.DMA((22,)),
         ],
         compiler_params=pltpu.CompilerParams(
-            collective_id=0, has_side_effects=True, vmem_limit_bytes=48 * 2**20
+            collective_id=0, has_side_effects=True, vmem_limit_bytes=58 * 2**20
         ),
         name="expert_layer",
     )(
-        tokens, cotangent, labels, domain_ids.reshape(1, n_tok),
+        tokens, cotangent, labels.reshape(1, n_tok), domain_ids.reshape(1, n_tok),
         domain_weights.reshape(1, -1), gate_weight, up_weight, down_weight,
     )
-    whole_act = pl.BlockSpec((n_rows, hid), lambda f: (0, 0))
-    dg, du, dd = pl.pallas_call(
-        weight_grad_kernel,
-        grid=(n_feat,),
-        out_shape=(
-            jax.ShapeDtypeStruct(gate_weight.shape, BF16),
-            jax.ShapeDtypeStruct(up_weight.shape, BF16),
-            jax.ShapeDtypeStruct(down_weight.shape, BF16),
-        ),
-        in_specs=[
-            pl.BlockSpec((1, 1, n_rows, width), lambda f: (0, f, 0, 0)),
-            pl.BlockSpec((1, 1, n_rows, width), lambda f: (1, f, 0, 0)),
-            whole_act, whole_act, whole_act,
+    return pl.pallas_call(
+        home_kernel,
+        out_shape=(out, out) + grads,
+        in_specs=[hbm] * 5,
+        out_specs=(vmem, vmem, hbm, hbm, hbm),
+        scratch_shapes=[
+            pltpu.VMEM((n_tok, n_lang * cap), BF16),
+            slab,
+            pltpu.VMEM(gate_weight.shape, BF16),
+            pltpu.VMEM(up_weight.shape, BF16),
+            pltpu.VMEM(down_weight.shape, BF16),
+            pltpu.SemaphoreType.DMA((26,)),
         ],
-        out_specs=(
-            pl.BlockSpec((1, width, hid), lambda f: (0, f, 0)),
-            pl.BlockSpec((1, width, hid), lambda f: (0, f, 0)),
-            pl.BlockSpec((1, hid, width), lambda f: (0, 0, f)),
-        ),
-        compiler_params=pltpu.CompilerParams(vmem_limit_bytes=32 * 2**20),
-        name="weight_grads",
-    )(rows, rows, hidden, ggp, gup)
-    return (y, yg, dg, du, dd)
+        compiler_params=pltpu.CompilerParams(vmem_limit_bytes=58 * 2**20),
+        name="home",
+    )(*parts)
 
 
 def solution(mesh):

time: 76.3 us -> 64.9 us (0.85)
  local copies, waits for them, and re-layouts: 8.96 us -> 0 us
  Pallas kernels: 66.5 us -> 64.1 us
    unnamed x15 -> x0, local copies, waits for them, and re-layouts: 8.96 us -> none
    pallas_call x2, Pallas kernels: 66.5 us -> 64.1 us  [the longest x1 57.7 us: fused_body(): pl.pallas_call(expert_kernel, out_shape=(jax.ShapeDtypeStruct((n_tok, n_l...]
where the time goes in v2:
time: 64.9 us; the launch traced here: 64.8 us
  Pallas kernels  64.1 us (99%)
    pallas_call x1, Pallas kernels, fused_body(): pl.pallas_call(expert_kernel, out_shape=(jax.ShapeDtypeStruct((n_tok, n_l...  57.7 us
    pallas_call x1, Pallas kernels, fused_body(): pl.pallas_call(home_kernel, out_shape=(out, out) + grads, in_specs=[hbm]...  6.39 us

profile of v2, /device:TPU:0, one launch (start us, length us, event | category | flops | bytes accessed | tf_op | source)
XLA Modules:
  0.0 64.8 jit_solution(817960488291117642)
XLA Ops:
  0.6 57.7 %expert_layer.1 = (bf16[128,256]{1,0:T(8,128)(2,1)}, bf16[2,4,64,512]{3,2,1,0:T(8,128)(2,1)}, bf16[1,2048,512]{2,1,0:T(8,128)(2,1)}, bf16[1,2048,512]{2,1,0:T(8,128)(2,1)}, bf16[1,512,2048]{2,1,0:T(8,128)(2,1)}) custom-call(bf16[128,512]{1,0:T(8,128)(2,1)} %tok_hbm.1, bf16[128,512]{1,0:T(8,128)(2,1)} %cot_hbm.1, s32[1,128]{1,0:T(1,128)} %bitcast.3, ...), custom_call_target="tpu_custom_call" | custom-call | tf_op jit(solution)/shard_map/expert_layer/pallas_call | solution.py:462
  58.4 6.4 %home.1 = (bf16[128,512]{1,0:T(8,128)(2,1)}, bf16[128,512]{1,0:T(8,128)(2,1)}, bf16[1,2048,512]{2,1,0:T(8,128)(2,1)}, bf16[1,2048,512]{2,1,0:T(8,128)(2,1)}, bf16[1,512,2048]{2,1,0:T(8,128)(2,1)}) custom-call(bf16[128,256]{1,0:T(8,128)(2,1)} %get-tuple-element.10.map_hbm, bf16[2,4,64,512]{3,2,1,0:T(8,128)(2,1)} %get-tuple-element.11.back_hbm, ...), custom_call_target="tpu_custom_call" | custom-call | tf_op jit(solution)/shard_map/home/pallas_call | solution.py:507

commit v3 on v2

--- a/solution.py
+++ b/solution.py
@@ -221,7 +221,7 @@
         jnp.where(dom_lane == column(dom_ref), dw_row, 0.0), axis=1, keepdims=True
     )
 
-    order = [(0, 0), (1, 0), (0, 1), (0, 2), (0, 3), (1, 1), (1, 2), (1, 3)]
+    order = [(0, 0), (1, 0), (0, 1), (0, 2), (0, 3), (1, 2), (1, 3), (1, 1)]
 
     def g0(q):
         k, j = order[q]
@@ -381,22 +381,23 @@
     g1(6), g2(5), g3(4), r1(0)
     forward(1)
     g1(7), g2(6), g3(5), r1(1)
-    backward(0)
     r2(0), r2(1)
     sums(0, 1)
-    g2(7), g3(6), g3(7), r1(2), r1(3)
+    g2(7), g3(6), r1(2), r1(3)
+    backward(1)
+    sums(1, 1)
+    g3(7)
+    r3(0), r3(1), r2(2), r2(3), r1(6), r1(7)
+    backward(0)
+    r3(2), r3(3), r2(6), r2(7)
     sums(1, 0)
-    r3(0), r3(1), r2(2), r2(3), r1(4), r1(5)
-    backward(1)
-    r3(2), r3(3), r2(4), r2(5)
-    sums(1, 1)
-    r1(6), r1(7), r3(4), r3(5)
+    r1(5), r1(4), r3(6), r3(7)
     weight_grad(2, 0), weight_grad(2, 1)
-    r2(6), r2(7)
+    r2(5), r2(4)
     for f in range(2, n_feat):
         weight_grad(2, f)
     weight_grad(0, 0)
-    r3(6), r3(7)
+    r3(5), r3(4)
     for f in range(1, n_feat):
         weight_grad(0, f)
     for f in range(n_feat):

time: 64.9 us -> 63 us (0.971)
  Pallas kernels: 64.1 us -> 62.2 us
    pallas_call x1, Pallas kernels: 57.7 us -> 55.8 us  [fused_body(): pl.pallas_call(expert_kernel, out_shape=(jax.ShapeDtypeStruct((n_tok, n_l...]
where the time goes in v3:
time: 63 us; the launch traced here: 62.8 us
  Pallas kernels  62.2 us (99%)
  between operations  0.64 us (1%)
    pallas_call x1, Pallas kernels, fused_body(): pl.pallas_call(expert_kernel, out_shape=(jax.ShapeDtypeStruct((n_tok, n_l...  55.8 us
    pallas_call x1, Pallas kernels, fused_body(): pl.pallas_call(home_kernel, out_shape=(out, out) + grads, in_specs=[hbm]...  6.39 us

profile of v3, /device:TPU:0, one launch (start us, length us, event | category | flops | bytes accessed | tf_op | source)
XLA Modules:
  0.0 62.8 jit_solution(141109315297975402)
XLA Ops:
  0.6 55.8 %expert_layer.1 = (bf16[128,256]{1,0:T(8,128)(2,1)}, bf16[2,4,64,512]{3,2,1,0:T(8,128)(2,1)}, bf16[1,2048,512]{2,1,0:T(8,128)(2,1)}, bf16[1,2048,512]{2,1,0:T(8,128)(2,1)}, bf16[1,512,2048]{2,1,0:T(8,128)(2,1)}) custom-call(bf16[128,512]{1,0:T(8,128)(2,1)} %tok_hbm.1, bf16[128,512]{1,0:T(8,128)(2,1)} %cot_hbm.1, s32[1,128]{1,0:T(1,128)} %bitcast.3, ...), custom_call_target="tpu_custom_call" | custom-call | tf_op jit(solution)/shard_map/expert_layer/pallas_call | solution.py:463
  56.4 6.4 %home.1 = (bf16[128,512]{1,0:T(8,128)(2,1)}, bf16[128,512]{1,0:T(8,128)(2,1)}, bf16[1,2048,512]{2,1,0:T(8,128)(2,1)}, bf16[1,2048,512]{2,1,0:T(8,128)(2,1)}, bf16[1,512,2048]{2,1,0:T(8,128)(2,1)}) custom-call(bf16[128,256]{1,0:T(8,128)(2,1)} %get-tuple-element.10.map_hbm, bf16[2,4,64,512]{3,2,1,0:T(8,128)(2,1)} %get-tuple-element.11.back_hbm, ...), custom_call_target="tpu_custom_call" | custom-call | tf_op jit(solution)/shard_map/home/pallas_call | solution.py:508
